TPU v7x, 32 devices: a whole 2x2x4 slice. The times are simulated.
32 devices in a mesh: leaf: 4 (over z), expert: 4 (over y, x), tensor: 2 (over core).
Axes of the slice: x: 2, y: 2, z: 4, core: 2. Of those that a mesh axis runs over, the one named last changes fastest.
Arguments:
- drafts: bfloat16 [1024, 6144], P('leaf', ('expert', 'tensor')), may hold values from -6 to 6
- children: bfloat16 [2048, 6144], P('leaf', ('expert', 'tensor')), may hold values from -6 to 6
- child_order: int32 [8], replicated, may hold values from 0 to 7, each once
- spans: int32 [2048], P('leaf'), may hold values from 0 to 15
- span_bias: float32 [48, 16], P(('expert', 'tensor')), may hold values from -4 to 4
- out_weight: bfloat16 [6144, 6144], P(('expert', 'tensor')), may hold values from -0.078125 to 0.078125
- norm_gain: float32 [6144], replicated, may hold values from 0.1 to 1.9
- router: bfloat16 [6144, 4], replicated, may hold values from -0.078125 to 0.078125
- routes: int32 [1024, 2], P(('leaf', 'expert')), may hold values from 0 to 3, all different within a row; in each aligned block of 64 rows (0 to 63, 64 to 127, ...) at most 64 rows name the same one
- w_gate: bfloat16 [4, 6144, 8192], P('expert', None, ('leaf', 'tensor')), may hold values from -0.078125 to 0.078125
- w_up: bfloat16 [4, 6144, 8192], P('expert', None, ('leaf', 'tensor')), may hold values from -0.078125 to 0.078125
- w_down: bfloat16 [4, 8192, 6144], P('expert', ('leaf', 'tensor')), may hold values from -0.0625 to 0.0625
Outputs:
- merged_out: float32 [1024, 6144], P(('leaf', 'expert'))
Inputs may be any that keep to these rules, and one draw needn't show every extreme that they name: `routes`: each row names two different experts; within the rows of one index pair of leaf and expert (64 aligned rows) no expert is named more than 64 times, and exactly 64 times in some of them. `child_order`: A permutation: every parent has exactly two children.
All inputs are finite; a program needn't handle non-finite values.
Results may differ from a plain program's by a relative error of at most 0.013.
Values may be sent and summed in bfloat16 or wider, within the bound.
A program may use at most 128 MiB of HBM per device.

v0:
```python
import math

import jax
import jax.numpy as jnp
from jax import lax
from jax.sharding import PartitionSpec as P

R = 256
PAR_DEV = 1


def per_device(
    drafts,
    children,
    child_order,
    spans,
    span_bias,
    out_weight,
    norm_gain,
    router,
    routes,
    w_gate,
    w_up,
    w_down,
):
    local_rows, local_width = drafts.shape
    heads_here = span_bias.shape[0]
    head_size = local_width // heads_here
    span_count = span_bias.shape[1]
    width = out_weight.shape[1]
    scale = 1.0 / math.sqrt(head_size)
    leaf_index = lax.axis_index("leaf")
    query_parent = leaf_index * PAR_DEV + jnp.arange(local_rows, dtype=jnp.int32) // R
    queries = drafts.reshape(local_rows, heads_here, head_size)
    bias_table = span_bias.T
    run_max = jnp.full((heads_here, local_rows), -1e30, jnp.float32)
    keys = lax.all_gather(children, "leaf", axis=0, tiled=True)
    key_spans = lax.all_gather(spans, "leaf", axis=0, tiled=True)
    key_count = keys.shape[0]
    child_ids = jnp.arange(key_count, dtype=jnp.int32) // R
    key_parent = jnp.take(child_order, child_ids) // 2
    key_heads = keys.reshape(key_count, heads_here, head_size)
    scores = (
        jnp.einsum("qhd,khd->hqk", queries, key_heads, preferred_element_type=jnp.float32) * scale
    )
    span_hot = (key_spans[:, None] == jnp.arange(span_count, dtype=jnp.int32)[None, :]).astype(
        jnp.float32
    )
    bias = jnp.dot(span_hot, bias_table, precision=lax.Precision.HIGHEST)
    scores = scores + bias.T[:, None, :]
    allowed = (query_parent[:, None] == key_parent[None, :])[None, :, :]
    masked = jnp.where(allowed, scores, -1e30)
    new_max = jnp.maximum(run_max, jnp.max(masked, axis=-1))
    weights = jnp.where(allowed, jnp.exp(masked - new_max[..., None]), 0.0)
    new_total = jnp.sum(weights, axis=-1)
    values = jnp.einsum(
        "hqk,khd->hqd", weights, key_heads.astype(jnp.float32), precision=lax.Precision.HIGHEST
    )
    attended = (
        (values / new_total[..., None])
        .transpose(1, 0, 2)
        .reshape(local_rows, local_width)
        .astype(jnp.bfloat16)
    )
    term = jnp.dot(attended, out_weight, preferred_element_type=jnp.float32)
    offset = lax.axis_index(("expert", "tensor")) * local_width
    own_cols = lax.dynamic_slice(term, (0, offset), (local_rows, local_width)) + drafts.astype(
        jnp.float32
    )
    term = lax.dynamic_update_slice(term, own_cols, (0, offset))
    share = lax.psum_scatter(term, ("expert", "tensor"), scatter_dimension=0, tiled=True)
    merged = lax.all_gather(share, "tensor", axis=0, tiled=True)
    mean_square = jnp.mean(merged * merged, axis=-1, keepdims=True)
    normed = (merged * lax.rsqrt(mean_square + 1e-05) * norm_gain).astype(jnp.bfloat16)
    logits = jnp.dot(normed, router, preferred_element_type=jnp.float32)
    experts = router.shape[1]
    tok_count = routes.shape[0]
    capacity = 4 * tok_count // lax.axis_size("expert")
    choice_hot = routes[:, :, None] == jnp.arange(experts, dtype=jnp.int32)[None, None, :]
    chosen = jnp.sum(jnp.where(choice_hot, logits[:, None, :], 0.0), axis=-1)
    gates = jax.nn.softmax(chosen, axis=-1)
    pairs = routes.reshape(-1)
    pair_hot = (pairs[:, None] == jnp.arange(experts, dtype=jnp.int32)[None, :]).astype(jnp.int32)
    earlier = jnp.cumsum(pair_hot, axis=0) - pair_hot
    slot_index = jnp.sum(earlier * pair_hot, axis=1)
    target = pairs * capacity + slot_index
    place_hot = (
        jnp.arange(experts * capacity, dtype=jnp.int32)[:, None] == target[None, :]
    ).astype(jnp.bfloat16)
    place_rows = jnp.sum(place_hot.reshape(experts * capacity, tok_count, 2), axis=-1)
    outgoing = jnp.dot(place_rows, normed, preferred_element_type=jnp.float32).astype(jnp.bfloat16)
    outgoing = outgoing.reshape(experts, capacity, width)
    arrived = lax.all_to_all(outgoing, "expert", split_axis=0, concat_axis=0, tiled=True).reshape(
        -1, width
    )
    piece = lax.all_gather(arrived, "leaf", axis=0, tiled=True)
    gate_v = jnp.dot(piece, w_gate[0], preferred_element_type=jnp.float32)
    up_v = jnp.dot(piece, w_up[0], preferred_element_type=jnp.float32)
    hidden = (jax.nn.silu(gate_v) * up_v).astype(jnp.bfloat16)
    part_rows = lax.psum_scatter(
        jnp.dot(hidden, w_down[0], preferred_element_type=jnp.float32).astype(jnp.bfloat16),
        ("leaf", "tensor"),
        scatter_dimension=0,
        tiled=True,
    )
    returned = lax.all_gather(part_rows, "tensor", axis=0, tiled=True)
    back = lax.all_to_all(
        returned.reshape(-1, capacity, width), "expert", split_axis=0, concat_axis=0, tiled=True
    ).reshape(-1, width)
    picked = jnp.take(back, target, axis=0).astype(jnp.float32).reshape(tok_count, 2, width)
    mixed = gates[:, 0:1] * picked[:, 0] + gates[:, 1:2] * picked[:, 1]
    return merged + mixed


def solution(mesh):
    in_specs = (
        P("leaf", ("expert", "tensor")),
        P("leaf", ("expert", "tensor")),
        P(),
        P("leaf"),
        P(("expert", "tensor"), None),
        P(("expert", "tensor"), None),
        P(),
        P(),
        P(("leaf", "expert"), None),
        P("expert", None, ("leaf", "tensor")),
        P("expert", None, ("leaf", "tensor")),
        P("expert", ("leaf", "tensor"), None),
    )
    out_specs = P(("leaf", "expert"), None)
    return jax.shard_map(
        per_device, mesh=mesh, in_specs=in_specs, out_specs=out_specs, check_vma=False
    )
```

profile of v0, /device:TPU:0, one launch (start us, length us, event | category | flops | bytes accessed | tf_op | source)
XLA Modules:
  0.0 685.6 jit_solution(15932585155562427533)
XLA Ops:
  6.5 0.0 copy-start
  6.5 0.0 all-gather.6.cloned.1.call-start
  6.5 2.3 copy.50
  8.8 0.0 all-gather.6.cloned.1.call-update
  8.9 0.0 reduce-scatter.3.cloned.1.call-start
  8.9 1.2 copy.49
  10.1 13.7 %all-gather = s32[4,1,512]{2,1,0:T(1,128)S(1)} all-gather(s32[1,1,512]{2,1,0:T(1,128)} %bitcast.86), channel_id=1, replica_groups=mesh['leaf'=4,'expert'=4,'tensor'=2] {'leaf'}, dimensions={0}, use_global_device_ids=true | all-gather | bytes 10240 | tf_op jit(solution)/shard_map/all_gather | solution.py:38
  23.8 1.6 fusion.50
  25.5 4.2 compare_select_fusion.1
  29.7 0.7 add_select_fusion.1
  30.4 1.6 convolution_bitcast_fusion
  32.0 0.4 broadcast_compare_fusion
  32.4 42.8 %all-gather.6.cloned.1.call-done = bf16[2048,768]{0,1:T(8,128)(2,1)} async-done(((bf16[512,768]{0,1:T(8,128)(2,1)}), bf16[2048,768]{0,1:T(8,128)(2,1)}) %all-gather.6.cloned.1.call-update) | async-done | bytes 3145744 | tf_op jit(solution)/shard_map/all_gather | solution.py:37
  75.2 4.6 fusion.9
  79.8 0.0 copy-start.6
  79.8 0.0 slice-start
  79.8 5.0 fusion.10
  84.8 0.0 copy-done.6
  84.8 0.0 slice-start.1
  84.8 0.0 slice-start.2
  84.8 10.1 %fusion.27 = bf16[256,6,128]{0,2,1:T(8,128)(2,1)S(1)} fusion(bf16[2048,6,128]{0,2,1:T(8,128)(2,1)S(1)} %bitcast.88, f32[6,256,2048]{2,1,0:T(8,128)S(1)} %get-tuple-element.18, f32[6,256]{1,0:T(8,128)S(1)} %broadcast_maximum_fusion, f32[6,2048]{1,0:T(8,128)S(1)} %convolution_bitcast_fusion, pred[256,2048]{1,0:T(8,128)(4,1)S(1)} %broadcast_compare_fusion, ...), kind=kOutput, calls=%fused_computation.36 | convolution fusion | flops 4847960064 | bytes 16707584 | tf_op jit(solution)/shard_map/hqk,khd->hqd/dot_general | solution.py:56
  94.9 0.0 slice-done
  94.9 0.0 slice-done.1
  95.0 0.0 copy-start.2
  95.0 4.6 fusion.51
  99.6 2.1 add_dynamic-update-slice_fusion
  101.7 0.0 reduce-scatter.3.cloned.1.call-update
  101.7 0.0 all-gather.8.cloned.1.call-start
  101.8 60.6 %reduce-scatter.3.cloned.1.call-done = f32[32,6144]{1,0:T(8,128)} async-done(((f32[256,6144]{1,0:T(8,128)}), f32[32,6144]{1,0:T(8,128)}) %reduce-scatter.3.cloned.1.call-update) | async-done | bytes 786448 | tf_op jit(solution)/shard_map/reduce_scatter | solution.py:71
  162.4 0.0 all-gather.8.cloned.1.call-update
  162.4 0.3 all-gather.10.cloned.1.call-start
  162.7 0.1 copy.53
  162.8 0.1 reshape.230
  162.9 0.1 fusion.31
  163.0 0.2 reduce_window_sum.11
  163.2 0.2 select_reduce_fusion
  163.4 0.1 reduce_sum.66
  163.5 0.1 copy.54
  163.6 0.1 fusion.30
  163.7 10.1 %all-gather.8.cloned.1.call-done = f32[64,6144]{1,0:T(8,128)} async-done(((f32[32,6144]{1,0:T(8,128)}), f32[64,6144]{1,0:T(8,128)}) %all-gather.8.cloned.1.call-update) | async-done | bytes 1572880 | tf_op jit(solution)/shard_map/all_gather | solution.py:72
  173.9 1.6 multiply_reduce_fusion
  175.5 2.4 convolution_convert_fusion
  177.9 40.9 %all_to_all.10 = bf16[4,64,6144]{2,1,0:T(8,128)(2,1)} all-to-all(bf16[4,64,6144]{2,1,0:T(8,128)(2,1)S(1)} %bitcast.77), channel_id=1, replica_groups=mesh['leaf'=4,'expert'=4,'tensor'=2] {'expert'}, dimensions={0} | all-to-all | bytes 6291456 | tf_op jit(solution)/shard_map/all_to_all | solution.py:93
  218.8 0.0 all-gather.10.cloned.1.call-update
  218.9 0.0 reduce-scatter.5.cloned.1.call-start
  218.9 217.8 %all-gather.10.cloned.1.call-done = bf16[1024,6144]{1,0:T(8,128)(2,1)} async-done(((bf16[256,6144]{1,0:T(8,128)(2,1)}), bf16[1024,6144]{1,0:T(8,128)(2,1)}) %all-gather.10.cloned.1.call-update) | async-done | bytes 12582928 | tf_op jit(solution)/shard_map/all_gather | solution.py:96
  436.7 17.2 %fusion.2 = f32[1024,1024]{1,0:T(8,128)S(1)} fusion(bf16[1024,6144]{1,0:T(8,128)(2,1)} %all-gather.10.cloned.1.call-done, bf16[1,6144,1024]{2,1,0:T(8,128)(2,1)} %param.22), kind=kOutput, calls=%fused_computation.3 | convolution fusion | flops 12884901888 | bytes 29360128 | tf_op jit(solution)/shard_map/dot_general | solution.py:98
  454.0 15.8 %multiply_convert_fusion = bf16[1024,1024]{1,0:T(8,128)(2,1)S(1)} fusion(f32[1024,1024]{1,0:T(8,128)S(1)} %fusion.2, bf16[1024,6144]{1,0:T(8,128)(2,1)S(1)} %copy-done.5, bf16[1,6144,1024]{2,1,0:T(8,128)(2,1)} %param.21), kind=kOutput, calls=%fused_computation.20 | convolution fusion | flops 12891193344 | bytes 31457280 | tf_op jit(solution)/shard_map/dot_general | solution.py:97
  469.8 19.9 %fusion.6 = bf16[1024,6144]{1,0:T(8,128)(2,1)} fusion(bf16[1024,1024]{1,0:T(8,128)(2,1)S(1)} %multiply_convert_fusion, bf16[1,1024,6144]{2,1,0:T(8,128)(2,1)} %param.23), kind=kOutput, calls=%fused_computation.9 | convolution fusion | flops 12891193344 | bytes 27262976 | tf_op jit(solution)/shard_map/dot_general | solution.py:101
  489.7 0.0 reduce-scatter.5.cloned.1.call-update
  489.8 0.0 all-gather.12.cloned.1.call-start
  489.8 127.5 %reduce-scatter.5.cloned.1.call-done = bf16[128,6144]{1,0:T(8,128)(2,1)} async-done(((bf16[1024,6144]{1,0:T(8,128)(2,1)}), bf16[128,6144]{1,0:T(8,128)(2,1)}) %reduce-scatter.5.cloned.1.call-update) | async-done | bytes 1572880 | tf_op jit(solution)/shard_map/reduce_scatter | solution.py:100
  617.3 0.0 all-gather.12.cloned.1.call-update
  617.3 12.0 %all-gather.12.cloned.1.call-done = bf16[256,6144]{1,0:T(8,128)(2,1)} async-done(((bf16[128,6144]{1,0:T(8,128)(2,1)}), bf16[256,6144]{1,0:T(8,128)(2,1)}) %all-gather.12.cloned.1.call-update) | async-done | bytes 3145744 | tf_op jit(solution)/shard_map/all_gather | solution.py:106
  629.3 4.0 all-to-all-start.1
  633.3 0.1 copy.55
  633.4 0.1 mul.100
  633.6 1.8 fusion.48
  635.5 34.6 %all-to-all-done.1 = bf16[4,64,6144]{2,1,0:T(8,128)(2,1)S(1)} async-done(((bf16[4,64,6144]{2,1,0:T(8,128)(2,1)}), bf16[4,64,6144]{2,1,0:T(8,128)(2,1)S(1)}, u32[]{:S(2)}, u32[]{:S(2)}) %all-to-all-start.1) | async-done | bytes 3145760 | tf_op jit(solution)/shard_map/all_to_all | solution.py:107
  670.1 2.6 gather_fusion
  672.7 3.5 gather.12
  676.3 1.0 fusion.24
  677.3 0.0 copy-done.1
  677.3 1.4 fusion.22
  (24 shorter events, 0.2 us)
Async XLA Ops:
  6.5 627.0 %copy-start = (bf16[6144,4]{0,1:T(4,128)(2,1)S(1)}, bf16[6144,4]{0,1:T(4,128)(2,1)}, u32[]{:S(2)}) copy-start(bf16[6144,4]{0,1:T(4,128)(2,1)} %param.19) | copy-start | bytes 147460
  6.5 68.6 %all-gather.6.cloned.1.call-start = ((), (), s32[]{:S(2)}) async-start(), calls=%async_computation.4 | async-start | bytes 3932160 | tf_op jit(solution)/shard_map/all_gather | solution.py:37
  8.9 153.5 %reduce-scatter.3.cloned.1.call-start = ((), (), s32[]{:S(2)}) async-start(), calls=%async_computation.5 | async-start | bytes 7077888 | tf_op jit(solution)/shard_map/reduce_scatter | solution.py:71
  79.8 5.0 copy-start.6
  79.8 15.1 %slice-start = ((s8[9437184]{0:T(1024)(128)(4,1)}), s8[4194304]{0:T(1024)(128)(4,1)S(1)}, s32[]{:S(2)}) async-start(s8[9437184]{0:T(1024)(128)(4,1)} %bitcast.78), calls=%async_computation.10 | async-start | bytes 8388608
  84.8 10.2 %slice-start.1 = ((s8[9437184]{0:T(1024)(128)(4,1)}), s8[4194304]{0:T(1024)(128)(4,1)S(1)}, s32[]{:S(2)}) async-start(s8[9437184]{0:T(1024)(128)(4,1)} %bitcast.78), calls=%async_computation.11 | async-start | bytes 8388608
  84.8 10.2 %slice-start.2 = ((s8[9437184]{0:T(1024)(128)(4,1)}), s8[1048576]{0:T(1024)(128)(4,1)S(1)}, s32[]{:S(2)}) async-start(s8[9437184]{0:T(1024)(128)(4,1)} %bitcast.78), calls=%async_computation.12 | async-start | bytes 2097152
  95.0 4.6 copy-start.2
  99.6 63.1 %copy-start.4 = (s32[64,2]{0,1:T(2,128)S(1)}, s32[64,2]{0,1:T(2,128)}, u32[]{:S(2)}) copy-start(s32[64,2]{0,1:T(2,128)} %param.20) | copy-start | bytes 1540
  101.7 73.8 %copy-start.3 = (f32[6144]{0:T(1024)S(1)}, f32[6144]{0:T(1024)}, u32[]{:S(2)}) copy-start(f32[6144]{0:T(1024)} %param.18) | copy-start | bytes 73732
  101.7 72.1 %all-gather.8.cloned.1.call-start = ((), (), s32[]{:S(2)}) async-start(), calls=%async_computation.6 | async-start | bytes 2359296 | tf_op jit(solution)/shard_map/all_gather | solution.py:72
  162.4 274.3 %all-gather.10.cloned.1.call-start = ((), (), s32[]{:S(2)}) async-start(), calls=%async_computation.7 | async-start | bytes 15728640 | tf_op jit(solution)/shard_map/all_gather | solution.py:96
  218.9 398.5 %reduce-scatter.5.cloned.1.call-start = ((), (), s32[]{:S(2)}) async-start(), calls=%async_computation.8 | async-start | bytes 14155776 | tf_op jit(solution)/shard_map/reduce_scatter | solution.py:100
  436.7 17.3 %copy-start.5 = (bf16[1024,6144]{1,0:T(8,128)(2,1)S(1)}, bf16[1024,6144]{1,0:T(8,128)(2,1)}, u32[]{:S(2)}) copy-start(bf16[1024,6144]{1,0:T(8,128)(2,1)} %all-gather.10.cloned.1.call-done) | copy-start | bytes 37748740
  489.8 139.6 %all-gather.12.cloned.1.call-start = ((), (), s32[]{:S(2)}) async-start(), calls=%async_computation.9 | async-start | bytes 4718592 | tf_op jit(solution)/shard_map/all_gather | solution.py:106
  629.3 40.8 %all-to-all-start.1 = ((bf16[4,64,6144]{2,1,0:T(8,128)(2,1)}), bf16[4,64,6144]{2,1,0:T(8,128)(2,1)S(1)}, u32[]{:S(2)}, u32[]{:S(2)}) async-start(bf16[4,64,6144]{2,1,0:T(8,128)(2,1)} %bitcast.80), calls=%async_computation.3 | async-start | bytes 6291456 | tf_op jit(solution)/shard_map/all_to_all | solution.py:107
  672.7 4.6 copy-start.1
Sparse Core Ops, SparseCore 0:
  9.0 66.1 all-gather.5
  101.8 60.5 reduce-scatter.2
  164.0 9.7 all-gather.7
  219.0 217.7 all-gather.9
  489.9 127.3 reduce-scatter.4
  618.8 10.4 all-gather.11
where the time goes:
time: 686 us
  waiting for transfers between devices  506 us (74%)
  matrix products  78.1 us (11%)
  blocking collectives  54.6 us (8%)
  other arithmetic  17.1 us (2%)
  between operations  13.8 us (2%)
  local copies, waits for them, and re-layouts  12 us (2%)
    all_gather x1, waiting for transfers between devices, per_device(): piece = lax.all_gather(arrived, 'leaf', axis=0, tiled=True)  218 us
    reduce_scatter x1, waiting for transfers between devices, per_device(): lax.psum_scatter(jnp.dot(hidden, w_down[0], preferred_element_type=jnp.fl...  128 us
    reduce_scatter x1, waiting for transfers between devices, per_device(): lax.psum_scatter(term, ('expert', 'tensor'), scatter_dimension=0, tiled=T...  60.6 us
    all_gather x1, waiting for transfers between devices, per_device(): keys = lax.all_gather(children, 'leaf', axis=0, tiled=True)  42.8 us
    all_to_all x1, blocking collectives, per_device(): lax.all_to_all(outgoing, 'expert', split_axis=0, concat_axis=0, tiled=True)  40.9 us
    all_to_all x1, waiting for transfers between devices, per_device(): lax.all_to_all(returned.reshape(-1, capacity, width), 'expert', split_axi...  34.6 us
    dot_general x1, matrix products, per_device(): jnp.dot(hidden, w_down[0], preferred_element_type=jnp.float32)  19.9 us
    dot_general x1, matrix products, per_device(): up_v = jnp.dot(piece, w_up[0], preferred_element_type=jnp.float32)  17.2 us
  transfers between devices with their start and end apart: 7, of which 7 were waited for; matrix products, arithmetic and copies ran while one was open for 2% of the time, Pallas kernels for 0%

commit v1 on v0

v1 whole, which is shorter than its diff:
```python
import math

import jax
import jax.numpy as jnp
from jax import lax
from jax.experimental import pallas as pl
from jax.experimental.pallas import tpu as pltpu
from jax.sharding import PartitionSpec as P

R = 256


def attend_kernel(groups, halves, span_count, ids, bias_ref, q_ref, ka_ref, kb_ref, sa_ref, sb_ref, o_ref):
    head = pl.program_id(0)
    scale = 1.0 / math.sqrt(q_ref.shape[1])
    queries = q_ref[...]
    contract = (((1,), (1,)), ((), ()))

    def score(k_ref, s_ref):
        spans = s_ref[0]
        bias = jnp.zeros(spans.shape, jnp.float32)
        for span in range(span_count):
            bias = jnp.where(spans == span, bias_ref[head, span], bias)
        dots = lax.dot_general(queries, k_ref[...], contract, preferred_element_type=jnp.float32)
        return dots * scale + bias

    score_a = score(ka_ref, sa_ref)
    score_b = score(kb_ref, sb_ref)
    top = jnp.maximum(
        jnp.max(score_a, axis=-1, keepdims=True), jnp.max(score_b, axis=-1, keepdims=True)
    )
    weight_a = jnp.exp(score_a - top)
    weight_b = jnp.exp(score_b - top)
    total = jnp.sum(weight_a, axis=-1, keepdims=True) + jnp.sum(weight_b, axis=-1, keepdims=True)
    values = jnp.dot(
        weight_a.astype(jnp.bfloat16), ka_ref[...], preferred_element_type=jnp.float32
    ) + jnp.dot(weight_b.astype(jnp.bfloat16), kb_ref[...], preferred_element_type=jnp.float32)
    attended = (values / total).astype(jnp.bfloat16)
    rows = attended.shape[0] // (groups * halves)
    for group in range(groups):
        for half in range(halves):
            source = (group * halves + half) * rows
            target = (half * groups + group) * rows
            o_ref[target : target + rows, :] = attended[source : source + rows, :]


def attend(drafts, keys, spans, ids, span_bias, groups, halves):
    rows, width = drafts.shape
    heads = span_bias.shape[0]
    size = width // heads
    return pl.pallas_call(
        lambda *refs: attend_kernel(groups, halves, span_bias.shape[1], *refs),
        out_shape=jax.ShapeDtypeStruct((rows, width), jnp.bfloat16),
        grid_spec=pltpu.PrefetchScalarGridSpec(
            num_scalar_prefetch=1,
            grid=(heads,),
            in_specs=[
                pl.BlockSpec(memory_space=pltpu.SMEM),
                pl.BlockSpec((rows, size), lambda h, ids: (0, h)),
                pl.BlockSpec((R, size), lambda h, ids: (ids[0], h)),
                pl.BlockSpec((R, size), lambda h, ids: (ids[1], h)),
                pl.BlockSpec((1, 1, R), lambda h, ids: (ids[0], 0, 0)),
                pl.BlockSpec((1, 1, R), lambda h, ids: (ids[1], 0, 0)),
            ],
            out_specs=pl.BlockSpec((rows, size), lambda h, ids: (0, h)),
        ),
        cost_estimate=pl.CostEstimate(
            flops=8 * rows * R * width, bytes_accessed=8 * rows * width, transcendentals=2 * rows * R * heads
        ),
    )(ids, span_bias, drafts, keys, keys, spans, spans)


def per_device(
    drafts,
    children,
    child_order,
    spans,
    span_bias,
    out_weight,
    norm_gain,
    router,
    routes,
    w_gate,
    w_up,
    w_down,
):
    leaves = lax.axis_size("leaf")
    groups = lax.axis_size("expert")
    halves = lax.axis_size("tensor")
    width = out_weight.shape[1]
    rows = drafts.shape[0] // (groups * halves)
    swap = [(index, index ^ 1) for index in range(halves)]
    parent = lax.axis_index("leaf")
    expert = lax.axis_index("expert")
    half = lax.axis_index("tensor")

    keys = lax.all_gather(children, "leaf", axis=0, tiled=True)
    key_spans = lax.all_gather(spans, "leaf", axis=0, tiled=True).reshape(-1, 1, R)
    all_routes = lax.all_gather(routes, ("leaf", "expert"), axis=0, tiled=True)
    draft_rows = lax.all_to_all(
        drafts, ("expert", "tensor"), split_axis=0, concat_axis=1, tiled=True
    )
    places = jnp.arange(child_order.shape[0], dtype=jnp.int32)
    ids = jnp.stack(
        [
            jnp.sum(jnp.where(child_order == 2 * parent, places, 0)),
            jnp.sum(jnp.where(child_order == 2 * parent + 1, places, 0)),
        ]
    ).astype(jnp.int32)
    attended = attend(drafts, keys, key_spans, ids, span_bias, groups, halves)
    term = jnp.dot(attended, out_weight, preferred_element_type=jnp.float32).astype(jnp.bfloat16)
    term = lax.psum_scatter(term, "tensor", scatter_dimension=0, tiled=True)
    term = lax.psum_scatter(term, "expert", scatter_dimension=0, tiled=True)
    merged = draft_rows.astype(jnp.float32) + term.astype(jnp.float32)
    mean_square = jnp.mean(merged * merged, axis=-1, keepdims=True)
    normed = (merged * lax.rsqrt(mean_square + 1e-05) * norm_gain).astype(jnp.bfloat16)

    own = lax.all_gather(normed, "leaf", axis=0, tiled=True)
    own = lax.all_gather(own, "expert", axis=0, tiled=True)
    other = lax.ppermute(own, "tensor", swap)
    merged_all = lax.all_gather(merged, "tensor", axis=0, tiled=True)

    routes_at = all_routes.reshape(leaves, groups, halves, rows, 2).transpose(2, 1, 0, 3, 4)
    routes_at = routes_at.reshape(halves, -1, 2)

    def gate_of(block, which):
        named = lax.dynamic_index_in_dim(routes_at, which, 0, keepdims=False)
        logits = jnp.dot(block, router, preferred_element_type=jnp.float32)
        hot = named[:, :, None] == jnp.arange(router.shape[1], dtype=jnp.int32)[None, None, :]
        chosen = jnp.sum(jnp.where(hot, logits[:, None, :], 0.0), axis=-1)
        gates = jax.nn.softmax(chosen, axis=-1)
        return jnp.sum(jnp.where(named == expert, gates, 0.0), axis=-1, keepdims=True)

    def hidden_of(block):
        gate_v = jnp.dot(block, w_gate[0], preferred_element_type=jnp.float32)
        up_v = jnp.dot(block, w_up[0], preferred_element_type=jnp.float32)
        return (jax.nn.silu(gate_v) * up_v).astype(jnp.bfloat16)

    own_gate = gate_of(own, half)
    own_hidden = hidden_of(own)
    other_gate = gate_of(other, 1 - half)
    other_hidden = hidden_of(other)
    other_part = (
        jnp.dot(other_hidden, w_down[0], preferred_element_type=jnp.float32) * other_gate
    ).astype(jnp.bfloat16)
    returned = lax.ppermute(other_part, "tensor", swap)
    own_part = jnp.dot(own_hidden, w_down[0], preferred_element_type=jnp.float32) * own_gate
    part = (own_part + returned.astype(jnp.float32)).astype(jnp.bfloat16)
    part = lax.psum_scatter(part, "expert", scatter_dimension=0, tiled=True)
    part = lax.psum_scatter(part, "leaf", scatter_dimension=0, tiled=True)
    mixed = lax.all_gather(part, "tensor", axis=0, tiled=True)
    return merged_all + mixed.astype(jnp.float32)


def solution(mesh):
    in_specs = (
        P("leaf", ("expert", "tensor")),
        P("leaf", ("expert", "tensor")),
        P(),
        P("leaf"),
        P(("expert", "tensor"), None),
        P(("expert", "tensor"), None),
        P(),
        P(),
        P(("leaf", "expert"), None),
        P("expert", None, ("leaf", "tensor")),
        P("expert", None, ("leaf", "tensor")),
        P("expert", ("leaf", "tensor"), None),
    )
    out_specs = P(("leaf", "expert"), None)
    return jax.shard_map(
        per_device, mesh=mesh, in_specs=in_specs, out_specs=out_specs, check_vma=False
    )
```

time: 686 us -> 487 us (0.71)
  waiting for transfers between devices: 506 us -> 303 us
  blocking collectives: 54.6 us -> 69.3 us
  local copies, waits for them, and re-layouts: 12 us -> 0.35 us
  other arithmetic: 17.1 us -> 8.41 us
  matrix products: 78.1 us -> 85.1 us
    all_gather x3, waiting for transfers between devices: 240 us -> 116 us  [the longest x1 70.8 us: per_device(): own = lax.all_gather(own, 'expert', axis=0, tiled=True)]
    reduce_scatter x2 -> x4, waiting for transfers between devices: 188 us -> 136 us  [the longest x1 66.6 us: per_device(): part = lax.psum_scatter(part, 'expert', scatter_dimension=0, tiled=True)]
    all_gather x1 -> x3, blocking collectives: 13.7 us -> 57.3 us  [the longest x1 39.7 us: per_device(): all_routes = lax.all_gather(routes, ('leaf', 'expert'), axis=0, tiled=True)]
    all_to_all x1 -> x0, waiting for transfers between devices: 34.6 us -> none  [per_device(): lax.all_to_all(returned.reshape(-1, capacity, width), 'expert', split_axi...]
    all_to_all x1, blocking collectives: 40.9 us -> 12.1 us  [per_device(): lax.all_to_all(drafts, ('expert', 'tensor'), split_axis=0, concat_axis=1,...]
    gather x3 -> x0, local copies, waits for them, and re-layouts: 7.8 us -> none  [the longest x2 6.16 us: per_device(): jnp.take(back, target, axis=0).astype(jnp.float32)]
    dot_general x9, matrix products: 78.1 us -> 85.1 us  [the longest x2 26 us: hidden_of(): up_v = jnp.dot(block, w_up[0], preferred_element_type=jnp.float32)]
  transfers between devices with their start and end apart: 7 -> 10, of which waited for: 7 -> 8; matrix products, arithmetic and copies ran while one was open for 2% -> 6% of each run, Pallas kernels for 0% -> 0%
where the time goes in v1:
time: 487 us
  waiting for transfers between devices  303 us (62%)
  matrix products  85.1 us (17%)
  blocking collectives  69.3 us (14%)
  between operations  13.8 us (3%)
  other arithmetic  8.41 us (2%)
  Pallas kernels  6.16 us (1%)
    all_gather x1, waiting for transfers between devices, per_device(): own = lax.all_gather(own, 'expert', axis=0, tiled=True)  70.8 us
    reduce_scatter x1, waiting for transfers between devices, per_device(): part = lax.psum_scatter(part, 'expert', scatter_dimension=0, tiled=True)  66.6 us
    all_gather x1, waiting for transfers between devices, per_device(): keys = lax.all_gather(children, 'leaf', axis=0, tiled=True)  49.6 us
    all_gather x1, blocking collectives, per_device(): all_routes = lax.all_gather(routes, ('leaf', 'expert'), axis=0, tiled=True)  39.7 us
    all_gather x1, waiting for transfers between devices, per_device(): own = lax.all_gather(normed, 'leaf', axis=0, tiled=True)  37.2 us
    reduce_scatter x1, waiting for transfers between devices, per_device(): part = lax.psum_scatter(part, 'leaf', scatter_dimension=0, tiled=True)  36.9 us
    dot_general x2, matrix products, hidden_of(): up_v = jnp.dot(block, w_up[0], preferred_element_type=jnp.float32)  26 us
    reduce_scatter x1, waiting for transfers between devices, per_device(): term = lax.psum_scatter(term, 'expert', scatter_dimension=0, tiled=True)  23.1 us
  transfers between devices with their start and end apart: 10, of which 8 were waited for; matrix products, arithmetic and copies ran while one was open for 6% of the time, Pallas kernels for 0%

profile of v1, /device:TPU:0, one launch (start us, length us, event | category | flops | bytes accessed | tf_op | source)
XLA Modules:
  0.0 486.7 jit_solution(8559638517097929202)
XLA Ops:
  6.5 0.0 copy-start
  6.5 0.7 all-gather.7.cloned.1.call-update
  7.3 0.0 reduce-scatter.5.cloned.1.call-start
  7.3 15.0 %all-gather = s32[4,1,512]{2,1,0:T(1,128)} all-gather(s32[1,1,512]{2,1,0:T(1,128)} %bitcast.62), channel_id=1, replica_groups=mesh['leaf'=4,'expert'=4,'tensor'=2] {'leaf'}, dimensions={0}, use_global_device_ids=true | all-gather | bytes 10240 | tf_op jit(solution)/shard_map/all_gather | solution.py:98
  22.3 1.3 fusion.23
  23.7 1.9 pad_add_fusion.refs_0_
  25.6 49.6 %all-gather.7.cloned.1.call-done.refs_3_.refs_4_ = bf16[2048,768]{1,0:T(8,128)(2,1)} async-done(((bf16[512,768]{1,0:T(8,128)(2,1)}), bf16[2048,768]{1,0:T(8,128)(2,1)}) %all-gather.7.cloned.1.call-update) | async-done | bytes 3145744 | tf_op jit(solution)/shard_map/all_gather | solution.py:97
  75.2 6.2 %shard_map.118 = bf16[256,768]{1,0:T(8,128)(2,1)} custom-call(s32[2]{0:T(128)} %pad_add_fusion.refs_0_, f32[6,16]{1,0:T(8,128)} %refs_1_.1, bf16[256,768]{1,0:T(8,128)(2,1)} %refs_2_.1, bf16[2048,768]{1,0:T(8,128)(2,1)} %all-gather.7.cloned.1.call-done.refs_3_.refs_4_, bf16[2048,768]{1,0:T(8,128)(2,1)} %all-gather.7.cloned.1.call-done.refs_3_.refs_4_, ...), custom_call_target="tpu_custom_call" | custom-call | flops 402653184 | bytes 1572864 | tf_op jit(solution)/shard_map/pallas_call | solution.py:51
  81.3 8.1 %convolution_convert_fusion = bf16[256,6144]{1,0:T(8,128)(2,1)} fusion(bf16[256,768]{1,0:T(8,128)(2,1)} %shard_map.118, bf16[768,6144]{1,0:T(8,128)(2,1)} %param.17), kind=kOutput, calls=%fused_computation.14 | convolution fusion | flops 2417491968 | bytes 12976128 | tf_op jit(solution)/shard_map/dot_general | solution.py:111
  89.4 0.0 reduce-scatter.5.cloned.1.call-update
  89.5 0.0 reduce-scatter.7.cloned.1.call-start
  89.5 9.7 %reduce-scatter.5.cloned.1.call-done = bf16[128,6144]{1,0:T(8,128)(2,1)} async-done(((bf16[256,6144]{1,0:T(8,128)(2,1)}), bf16[128,6144]{1,0:T(8,128)(2,1)}) %reduce-scatter.5.cloned.1.call-update) | async-done | bytes 1572880 | tf_op jit(solution)/shard_map/reduce_scatter | solution.py:112
  99.2 0.0 reduce-scatter.7.cloned.1.call-update
  99.2 0.0 all-gather.11.cloned.1.call-start
  99.2 0.0 copy-done.3
  99.3 12.1 %all_to_all.13 = bf16[8,32,768]{2,1,0:T(8,128)(2,1)S(1)} all-to-all(bf16[8,32,768]{2,1,0:T(8,128)(2,1)S(1)} %bitcast.58), channel_id=1, replica_groups=mesh['leaf'=4,'expert'=4,'tensor'=2] {'expert','tensor'}, dimensions={0} | all-to-all | bytes 786432 | tf_op jit(solution)/shard_map/all_to_all | solution.py:100
  111.3 0.1 convert_bitcast_fusion
  111.4 0.1 copy.36
  111.4 23.1 %reduce-scatter.7.cloned.1.call-done = bf16[32,6144]{1,0:T(8,128)(2,1)} async-done(((bf16[128,6144]{1,0:T(8,128)(2,1)}), bf16[32,6144]{1,0:T(8,128)(2,1)}) %reduce-scatter.7.cloned.1.call-update) | async-done | bytes 393232 | tf_op jit(solution)/shard_map/reduce_scatter | solution.py:113
  134.6 1.2 multiply_reduce_fusion
  135.8 0.0 copy-done.4
  135.8 1.0 multiply_convert_fusion.4
  136.8 0.0 all-gather.11.cloned.1.call-update
  136.8 0.0 all-gather.13.cloned.1.call-start
  136.9 37.2 %all-gather.11.cloned.1.call-done = bf16[128,6144]{1,0:T(8,128)(2,1)} async-done(((bf16[32,6144]{1,0:T(8,128)(2,1)}), bf16[128,6144]{1,0:T(8,128)(2,1)}) %all-gather.11.cloned.1.call-update) | async-done | bytes 1572880 | tf_op jit(solution)/shard_map/all_gather | solution.py:118
  174.0 0.0 all-gather.13.cloned.1.call-update
  174.1 0.0 reduce-scatter.9.cloned.1.call-start
  174.1 70.8 %all-gather.13.cloned.1.call-done = bf16[512,6144]{1,0:T(8,128)(2,1)} async-done(((bf16[128,6144]{1,0:T(8,128)(2,1)}), bf16[512,6144]{1,0:T(8,128)(2,1)}) %all-gather.13.cloned.1.call-update) | async-done | bytes 6291472 | tf_op jit(solution)/shard_map/all_gather | solution.py:119
  244.9 0.0 collective-permute-start
  244.9 39.7 %all-gather.1 = s32[16,64,2]{1,2,0:T(2,128)S(1)} all-gather(s32[1,64,2]{1,2,0:T(2,128)S(1)} %bitcast.63), channel_id=1, replica_groups=mesh['leaf'=4,'expert'=4,'tensor'=2] {'leaf','expert'}, dimensions={0}, use_global_device_ids=true | all-gather | bytes 8704 | tf_op jit(solution)/shard_map/all_gather | solution.py:99
  284.6 0.1 reshape.36
  284.8 0.1 reshape.37
  284.9 0.0 collective-permute-done
  284.9 4.5 fusion.27
  289.5 0.0 slice-start.4
  289.5 0.0 slice-start.5
  289.5 0.0 slice-start
  289.6 12.8 %fusion.4 = f32[512,1024]{1,0:T(8,128)} fusion(bf16[512,6144]{1,0:T(8,128)(2,1)} %collective-permute-done, bf16[1,6144,1024]{2,1,0:T(8,128)(2,1)} %param.22), kind=kOutput, calls=%fused_computation.4 | convolution fusion | flops 6442450944 | bytes 20971520 | tf_op jit(solution)/shard_map/dot_general | solution.py:136
  302.4 12.6 %fusion.8 = f32[512,1024]{1,0:T(8,128)} fusion(bf16[512,6144]{1,0:T(8,128)(2,1)} %collective-permute-done, bf16[1,6144,1024]{2,1,0:T(8,128)(2,1)} %param.21), kind=kOutput, calls=%fused_computation.8 | convolution fusion | flops 6442450944 | bytes 20971520 | tf_op jit(solution)/shard_map/dot_general | solution.py:135
  315.0 11.0 %multiply_convert_fusion = bf16[512,6144]{1,0:T(8,128)(2,1)} fusion(bf16[1,1024,6144]{2,1,0:T(8,128)(2,1)S(1)} %bitcast.65, f32[512]{0:T(512)S(1)} %fusion.20, f32[512,1024]{1,0:T(8,128)} %fusion.4, f32[512,1024]{1,0:T(8,128)} %fusion.8), kind=kOutput, calls=%fused_computation.13 | convolution fusion | flops 6451888128 | bytes 23070720 | tf_op jit(solution)/shard_map/dot_general | solution.py:144
  326.1 0.0 collective-permute-start.1
  326.1 0.0 slice-start.2
  326.1 1.7 fusion.26
  327.9 0.0 slice-start.3
  327.9 0.0 slice-start.7
  328.0 0.0 slice-start.8
  328.0 13.2 %fusion.6 = f32[512,1024]{1,0:T(8,128)S(1)} fusion(bf16[512,6144]{1,0:T(8,128)(2,1)} %all-gather.13.cloned.1.call-done, bf16[1,6144,1024]{2,1,0:T(8,128)(2,1)} %param.22), kind=kOutput, calls=%fused_computation.6 | convolution fusion | flops 6442450944 | bytes 20971520 | tf_op jit(solution)/shard_map/dot_general | solution.py:136
  341.2 0.0 slice-start.9
  341.2 10.1 %multiply_convert_fusion.2 = bf16[512,1024]{1,0:T(8,128)(2,1)S(1)} fusion(f32[512,1024]{1,0:T(8,128)S(1)} %fusion.6, bf16[512,6144]{1,0:T(8,128)(2,1)S(1)} %bitcast.56, bf16[1,6144,1024]{2,1,0:T(8,128)(2,1)} %param.21), kind=kOutput, calls=%fused_computation.16 | convolution fusion | flops 6445596672 | bytes 22020096 | tf_op jit(solution)/shard_map/dot_general | solution.py:135
  351.3 0.0 collective-permute-done.1
  351.3 0.0 slice-done.7
  351.3 0.0 slice-done.8
  351.3 0.0 slice-done.9
  351.4 11.0 %add_convert_fusion = bf16[512,6144]{1,0:T(8,128)(2,1)} fusion(bf16[512,6144]{1,0:T(8,128)(2,1)} %collective-permute-done.1, bf16[512,1024]{1,0:T(8,128)(2,1)S(1)} %multiply_convert_fusion.2, bf16[1,1024,6144]{2,1,0:T(8,128)(2,1)S(1)} %bitcast.67, f32[512]{0:T(512)S(1)} %fusion.19), kind=kOutput, calls=%fused_computation.12 | convolution fusion | flops 6455033856 | bytes 26216448 | tf_op jit(solution)/shard_map/dot_general | solution.py:147
  362.3 0.0 reduce-scatter.9.cloned.1.call-update
  362.4 0.0 reduce-scatter.11.cloned.1.call-start
  362.4 66.6 %reduce-scatter.9.cloned.1.call-done = bf16[128,6144]{1,0:T(8,128)(2,1)} async-done(((bf16[512,6144]{1,0:T(8,128)(2,1)}), bf16[128,6144]{1,0:T(8,128)(2,1)}) %reduce-scatter.9.cloned.1.call-update) | async-done | bytes 1572880 | tf_op jit(solution)/shard_map/reduce_scatter | solution.py:149
  429.0 0.0 reduce-scatter.11.cloned.1.call-update
  429.0 0.0 all-gather.9.cloned.1.call-start
  429.1 0.7 all-gather.9.cloned.1.call-update
  429.8 36.9 %reduce-scatter.11.cloned.1.call-done = bf16[32,6144]{1,0:T(8,128)(2,1)} async-done(((bf16[128,6144]{1,0:T(8,128)(2,1)}), bf16[32,6144]{1,0:T(8,128)(2,1)}) %reduce-scatter.11.cloned.1.call-update) | async-done | bytes 393232 | tf_op jit(solution)/shard_map/reduce_scatter | solution.py:150
  466.7 2.6 all_gather.27
  469.3 7.9 %all-gather.9.cloned.1.call-done = f32[64,6144]{1,0:T(8,128)} async-done(((f32[32,6144]{1,0:T(8,128)}), f32[64,6144]{1,0:T(8,128)}) %all-gather.9.cloned.1.call-update) | async-done | bytes 1572880 | tf_op jit(solution)/shard_map/all_gather | solution.py:121
  477.1 2.7 convert_add_fusion
  (34 shorter events, 0.3 us)
Async XLA Ops:
  6.5 278.4 %copy-start = (bf16[6144,4]{0,1:T(4,128)(2,1)S(1)}, bf16[6144,4]{0,1:T(4,128)(2,1)}, u32[]{:S(2)}) copy-start(bf16[6144,4]{0,1:T(4,128)(2,1)} %param.19) | copy-start | bytes 147460
  6.5 68.6 %all-gather.7.cloned.1.call-start = ((), (), s32[]{:S(2)}) async-start(), calls=%async_computation.5 | async-start | bytes 3932160 | tf_op jit(solution)/shard_map/all_gather | solution.py:97
  7.3 91.9 %reduce-scatter.5.cloned.1.call-start = ((), (), s32[]{:S(2)}) async-start(), calls=%async_computation.6 | async-start | bytes 4718592 | tf_op jit(solution)/shard_map/reduce_scatter | solution.py:112
  81.3 17.9 %copy-start.3 = (bf16[256,768]{1,0:T(8,128)(2,1)S(1)}, bf16[256,768]{1,0:T(8,128)(2,1)}, u32[]{:S(2)}) copy-start(bf16[256,768]{1,0:T(8,128)(2,1)} %refs_2_.1) | copy-start | bytes 1179652
  89.4 46.4 %copy-start.4 = (f32[6144]{0:T(1024)S(1)}, f32[6144]{0:T(1024)}, u32[]{:S(2)}) copy-start(f32[6144]{0:T(1024)} %param.18) | copy-start | bytes 73732
  89.4 155.5 %copy-start.5 = (s32[64,2]{0,1:T(2,128)S(1)}, s32[64,2]{0,1:T(2,128)}, u32[]{:S(2)}) copy-start(s32[64,2]{0,1:T(2,128)} %param.20) | copy-start | bytes 1540
  89.5 45.1 %reduce-scatter.7.cloned.1.call-start = ((), (), s32[]{:S(2)}) async-start(), calls=%async_computation.7 | async-start | bytes 1966080 | tf_op jit(solution)/shard_map/reduce_scatter | solution.py:113
  99.2 74.8 %all-gather.11.cloned.1.call-start = ((), (), s32[]{:S(2)}) async-start(), calls=%async_computation.9 | async-start | bytes 1966080 | tf_op jit(solution)/shard_map/all_gather | solution.py:118
  135.8 166.6 %copy-start.2 = (f32[32,6144]{1,0:T(8,128)}, f32[32,6144]{1,0:T(8,128)S(1)}, u32[]{:S(2)}) copy-start(f32[32,6144]{1,0:T(8,128)S(1)} %get-tuple-element.8) | copy-start | bytes 2359300
  136.8 108.1 %all-gather.13.cloned.1.call-start = ((), (), s32[]{:S(2)}) async-start(), calls=%async_computation.10 | async-start | bytes 7864320 | tf_op jit(solution)/shard_map/all_gather | solution.py:119
  174.1 254.9 %reduce-scatter.9.cloned.1.call-start = ((), (), s32[]{:S(2)}) async-start(), calls=%async_computation.11 | async-start | bytes 7864320 | tf_op jit(solution)/shard_map/reduce_scatter | solution.py:149
  244.9 39.9 %collective-permute-start = (bf16[512,6144]{1,0:T(8,128)(2,1)}, bf16[512,6144]{1,0:T(8,128)(2,1)}, u32[]{:S(2)}, u32[]{:S(2)}) collective-permute-start(bf16[512,6144]{1,0:T(8,128)(2,1)} %all-gather.13.cloned.1.call-done), channel_id=1, source_target_pairs={{0,1},{1,0},{2,3},{3,2},{4,5},{5,4},{6,7},{7,6},{8,9},{9,8},{10,11... | collective-permute-start | bytes 18874376 | tf_op jit(solution)/shard_map/ppermute | solution.py:120
  289.5 25.5 %slice-start.4 = ((s8[12582912]{0:T(1024)(128)(4,1)}), s8[4194304]{0:T(1024)(128)(4,1)S(1)}, s32[]{:S(2)}) async-start(s8[12582912]{0:T(1024)(128)(4,1)} %bitcast.64), calls=%async_computation.17 | async-start | bytes 8388608
  289.5 25.5 %slice-start.5 = ((s8[12582912]{0:T(1024)(128)(4,1)}), s8[4194304]{0:T(1024)(128)(4,1)S(1)}, s32[]{:S(2)}) async-start(s8[12582912]{0:T(1024)(128)(4,1)} %bitcast.64), calls=%async_computation.18 | async-start | bytes 8388608
  289.5 36.5 %slice-start = ((s8[6291456]{0:T(1024)(128)(4,1)}), s8[4194304]{0:T(1024)(128)(4,1)S(1)}, s32[]{:S(2)}) async-start(s8[6291456]{0:T(1024)(128)(4,1)} %bitcast.53), calls=%async_computation.13 | async-start | bytes 8388608
  302.4 12.6 %slice-start.6 = ((s8[12582912]{0:T(1024)(128)(4,1)}), s8[4194304]{0:T(1024)(128)(4,1)S(1)}, s32[]{:S(2)}) async-start(s8[12582912]{0:T(1024)(128)(4,1)} %bitcast.64), calls=%async_computation.19 | async-start | bytes 8388608
  302.4 23.7 %slice-start.1 = ((s8[6291456]{0:T(1024)(128)(4,1)}), s8[2097152]{0:T(1024)(128)(4,1)S(1)}, s32[]{:S(2)}) async-start(s8[6291456]{0:T(1024)(128)(4,1)} %bitcast.53), calls=%async_computation.14 | async-start | bytes 4194304
  326.1 25.3 %collective-permute-start.1 = (bf16[512,6144]{1,0:T(8,128)(2,1)}, bf16[512,6144]{1,0:T(8,128)(2,1)}, u32[]{:S(2)}, u32[]{:S(2)}) collective-permute-start(bf16[512,6144]{1,0:T(8,128)(2,1)} %multiply_convert_fusion), channel_id=1, source_target_pairs={{0,1},{1,0},{2,3},{3,2},{4,5},{5,4},{6,7},{7,6},{8,9},{9,8},{10,11... | collective-permute-start | bytes 18874376 | tf_op jit(solution)/shard_map/ppermute | solution.py:146
  326.1 15.1 %slice-start.2 = ((s8[6291456]{0:T(1024)(128)(4,1)}), s8[2097152]{0:T(1024)(128)(4,1)S(1)}, s32[]{:S(2)}) async-start(s8[6291456]{0:T(1024)(128)(4,1)} %bitcast.55), calls=%async_computation.15 | async-start | bytes 4194304
  327.9 13.2 %slice-start.3 = ((s8[6291456]{0:T(1024)(128)(4,1)}), s8[4194304]{0:T(1024)(128)(4,1)S(1)}, s32[]{:S(2)}) async-start(s8[6291456]{0:T(1024)(128)(4,1)} %bitcast.55), calls=%async_computation.16 | async-start | bytes 8388608
  327.9 23.4 %slice-start.7 = ((s8[12582912]{0:T(1024)(128)(4,1)}), s8[4194304]{0:T(1024)(128)(4,1)S(1)}, s32[]{:S(2)}) async-start(s8[12582912]{0:T(1024)(128)(4,1)} %bitcast.66), calls=%async_computation.20 | async-start | bytes 8388608
  328.0 23.4 %slice-start.8 = ((s8[12582912]{0:T(1024)(128)(4,1)}), s8[4194304]{0:T(1024)(128)(4,1)S(1)}, s32[]{:S(2)}) async-start(s8[12582912]{0:T(1024)(128)(4,1)} %bitcast.66), calls=%async_computation.21 | async-start | bytes 8388608
  341.2 10.2 %slice-start.9 = ((s8[12582912]{0:T(1024)(128)(4,1)}), s8[4194304]{0:T(1024)(128)(4,1)S(1)}, s32[]{:S(2)}) async-start(s8[12582912]{0:T(1024)(128)(4,1)} %bitcast.66), calls=%async_computation.22 | async-start | bytes 8388608
  362.3 117.5 %copy-start.1 = (bf16[6144,4]{0,1:T(4,128)(2,1)S(1)}, bf16[6144,4]{0,1:T(4,128)(2,1)}, u32[]{:S(2)}) copy-start(bf16[6144,4]{0,1:T(4,128)(2,1)} %param.19) | copy-start | bytes 147460
  362.4 104.3 %reduce-scatter.11.cloned.1.call-start = ((), (), s32[]{:S(2)}) async-start(), calls=%async_computation.12 | async-start | bytes 1966080 | tf_op jit(solution)/shard_map/reduce_scatter | solution.py:150
  429.0 48.1 %all-gather.9.cloned.1.call-start = ((), (), s32[]{:S(2)}) async-start(), calls=%async_computation.8 | async-start | bytes 2359296 | tf_op jit(solution)/shard_map/all_gather | solution.py:121
Sparse Core Ops, SparseCore 0:
  8.9 66.1 all-gather.6
  89.6 9.5 reduce-scatter.4
  102.4 32.0 reduce-scatter.6
  136.9 37.0 all-gather.10
  175.9 69.0 all-gather.12
  362.5 66.4 reduce-scatter.8
  431.4 35.2 reduce-scatter.10
  468.3 8.7 all-gather.8

commit v2 on v1

--- a/solution.py
+++ b/solution.py
@@ -69,6 +69,213 @@
         ),
     )(ids, span_bias, drafts, keys, keys, spans, spans)
 
+MESH = pl.DeviceIdType.MESH
+
+
+def position():
+    leaf, expert, half = (lax.axis_index(name) for name in ("leaf", "expert", "tensor"))
+    across = expert + 1 - 2 * (expert % 2)
+    along = (expert + 2) % 4
+    return leaf, expert, half, across, along
+
+
+def greet(partners):
+    barrier = pltpu.get_barrier_semaphore()
+    for partner in partners:
+        pl.semaphore_signal(barrier, inc=1, device_id=partner, device_id_type=MESH)
+    pl.semaphore_wait(barrier, len(partners))
+
+
+def send(source, target, sems, index, device):
+    copy = pltpu.make_async_remote_copy(
+        src_ref=source,
+        dst_ref=target,
+        send_sem=sems.at[0, index],
+        recv_sem=sems.at[1, index],
+        device_id=device,
+        device_id_type=MESH,
+    )
+    copy.start()
+    return copy
+
+
+def gather_kernel(
+    leaves, rows, own_ref, merged_ref, all_ref, pair_ref, local, z_sem, x_sem, y_sem, a_sem, b_sem, swap_sem
+):
+    leaf, expert, half, across, along = position()
+    opposite = 3 - expert
+    x_dev, y_dev = (leaf, across, half), (leaf, along, half)
+    twin = (leaf, expert, 1 - half)
+    z_devs = [((leaf + step) % leaves, expert, half) for step in range(1, leaves)]
+    greet([x_dev, y_dev, twin] + z_devs)
+    part = rows // 2
+
+    def block(group, step, first=0, count=rows):
+        start = (group * leaves + (leaf + leaves - step) % leaves) * rows + first
+        return all_ref.at[half, pl.ds(pl.multiple_of(start, 16), count), :]
+
+    copies = []
+    keep = pltpu.make_async_copy(own_ref, block(expert, 0), local.at[0])
+    keep.start()
+    keep_pair = pltpu.make_async_copy(merged_ref, pair_ref.at[half], local.at[1])
+    keep_pair.start()
+    z_copies = [None]
+    for step in range(1, leaves):
+        z_copies.append(send(own_ref, block(expert, 0), z_sem, step, z_devs[step - 1]))
+    x_copies, y_copies, a_copies, b_copies = {}, {}, {}, {}
+    x_copies[0] = send(own_ref, block(expert, 0), x_sem, 0, x_dev)
+    y_copies[0] = send(own_ref, block(expert, 0), y_sem, 0, y_dev)
+    copies.append(send(own_ref, block(expert, 0), swap_sem, 0, twin))
+    copies.append(send(merged_ref, pair_ref.at[half], swap_sem, 4 * leaves, twin))
+    order = [0] + sorted(range(1, leaves), key=lambda step: min(step, leaves - step))
+
+    def forward(step):
+        x_copies[step].wait_recv()
+        a_copies[step] = send(
+            block(across, step, 0, part), block(across, step, 0, part), a_sem, step, y_dev
+        )
+        y_copies[step].wait_recv()
+        b_copies[step] = send(
+            block(along, step, part, part), block(along, step, part, part), b_sem, step, x_dev
+        )
+        copies.append(send(block(across, step), block(across, step), swap_sem, leaves + step, twin))
+        copies.append(send(block(along, step), block(along, step), swap_sem, 2 * leaves + step, twin))
+
+    for turn in range(1, leaves):
+        step = order[turn]
+        z_copies[step].wait_recv()
+        x_copies[step] = send(block(expert, step), block(expert, step), x_sem, step, x_dev)
+        y_copies[step] = send(block(expert, step), block(expert, step), y_sem, step, y_dev)
+        copies.append(send(block(expert, step), block(expert, step), swap_sem, step, twin))
+        forward(order[turn - 1])
+    forward(order[-1])
+    for step in order:
+        a_copies[step].wait_recv()
+        b_copies[step].wait_recv()
+        copies.append(
+            send(block(opposite, step), block(opposite, step), swap_sem, 3 * leaves + step, twin)
+        )
+    for copy in copies:
+        copy.wait()
+    for step in order:
+        for group in (x_copies, y_copies, a_copies, b_copies):
+            group[step].wait_send()
+        if step > 0:
+            z_copies[step].wait_send()
+    keep.wait()
+    keep_pair.wait()
+
+
+def gather_rows(normed, merged, leaves, groups):
+    rows, width = normed.shape
+    dma = pltpu.SemaphoreType.DMA
+    anywhere = pl.BlockSpec(memory_space=pl.ANY)
+    return pl.pallas_call(
+        lambda *refs: gather_kernel(leaves, rows, *refs),
+        out_shape=(
+            jax.ShapeDtypeStruct((2, groups * leaves * rows, width), normed.dtype),
+            jax.ShapeDtypeStruct((2, rows, width), merged.dtype),
+        ),
+        in_specs=[anywhere] * 2,
+        out_specs=(anywhere, anywhere),
+        scratch_shapes=[dma((2,))]
+        + [dma((2, leaves))] * 5
+        + [dma((2, 4 * leaves + 1))],
+        compiler_params=pltpu.CompilerParams(collective_id=1, has_side_effects=True),
+    )(normed, merged)
+
+
+def scatter_kernel(
+    leaves, rows, part_ref, out_ref, in_a, in_b, mid_a, mid_b, last_a, last_b, sums, far,
+    a_sem, b_sem, ma_sem, mb_sem, z_sem, swap_sem,
+):
+    leaf, expert, half, across, along = position()
+    opposite = 3 - expert
+    x_dev, y_dev = (leaf, across, half), (leaf, along, half)
+    twin = (leaf, expert, 1 - half)
+    z_devs = [((leaf + step) % leaves, expert, half) for step in range(1, leaves)]
+    greet([x_dev, y_dev, twin] + z_devs)
+    cut = rows // 2
+
+    def block(group, step, first):
+        start = (group * leaves + (leaf + step) % leaves) * rows + first
+        return part_ref.at[pl.ds(pl.multiple_of(start, 16), cut), :]
+
+    def wide(ref):
+        return ref[...].astype(jnp.float32)
+
+    order = list(range(1, leaves)) + [0]
+    first, second, third = {}, {}, {}
+    for step in order:
+        first[step] = (
+            send(block(opposite, step, 0), in_a.at[step, 1], a_sem, 2 * step + 1, x_dev),
+            send(block(opposite, step, cut), in_b.at[step, 1], b_sem, 2 * step + 1, y_dev),
+            send(block(across, step, 0), in_a.at[step, 0], a_sem, 2 * step, x_dev),
+            send(block(along, step, cut), in_b.at[step, 0], b_sem, 2 * step, y_dev),
+        )
+
+    def middle(step):
+        first[step][0].wait_recv()
+        mid_a[step] = (wide(block(along, step, 0)) + wide(in_a.at[step, 1])).astype(jnp.bfloat16)
+        to_y = send(mid_a.at[step], last_a.at[step], ma_sem, step, y_dev)
+        first[step][1].wait_recv()
+        mid_b[step] = (wide(block(across, step, cut)) + wide(in_b.at[step, 1])).astype(jnp.bfloat16)
+        to_x = send(mid_b.at[step], last_b.at[step], mb_sem, step, x_dev)
+        second[step] = (to_y, to_x)
+
+    def finish(step):
+        first[step][2].wait_recv()
+        first[step][3].wait_recv()
+        second[step][0].wait_recv()
+        sum_a = wide(block(expert, step, 0)) + wide(in_a.at[step, 0]) + wide(last_a.at[step])
+        sums[step, 0:cut, :] = sum_a.astype(jnp.bfloat16)
+        second[step][1].wait_recv()
+        sum_b = wide(block(expert, step, cut)) + wide(in_b.at[step, 0]) + wide(last_b.at[step])
+        sums[step, cut:rows, :] = sum_b.astype(jnp.bfloat16)
+        if step > 0:
+            third[step] = send(sums.at[step], far.at[step], z_sem, step, z_devs[step - 1])
+
+    for turn, step in enumerate(order):
+        middle(step)
+        if turn > 0:
+            finish(order[turn - 1])
+    finish(order[-1])
+    total = wide(sums.at[0])
+    for step in range(1, leaves):
+        third[step].wait_recv()
+        total = total + wide(far.at[step])
+    out_ref[half] = total.astype(jnp.bfloat16)
+    swapped = send(out_ref.at[half], out_ref.at[half], swap_sem, 0, twin)
+    for step in order:
+        for copy in first[step] + second[step]:
+            copy.wait_send()
+        if step > 0:
+            third[step].wait_send()
+    swapped.wait()
+
+
+def scatter_rows(part, leaves, groups):
+    rows, width = part.shape[0] // (leaves * groups), part.shape[1]
+    cut = rows // 2
+    dma = pltpu.SemaphoreType.DMA
+    kind = part.dtype
+    inside = pl.BlockSpec(memory_space=pltpu.VMEM)
+    return pl.pallas_call(
+        lambda *refs: scatter_kernel(leaves, rows, *refs),
+        out_shape=jax.ShapeDtypeStruct((2, rows, width), kind),
+        in_specs=[inside],
+        out_specs=inside,
+        scratch_shapes=[pltpu.VMEM((leaves, 2, cut, width), kind)] * 2
+        + [pltpu.VMEM((leaves, cut, width), kind)] * 4
+        + [pltpu.VMEM((leaves, rows, width), kind)] * 2
+        + [dma((2, 2 * leaves))] * 2
+        + [dma((2, leaves))] * 3
+        + [dma((2, 1))],
+        compiler_params=pltpu.CompilerParams(
+            collective_id=2, has_side_effects=True, vmem_limit_bytes=40 * 1024 * 1024
+        ),
+    )(part)
+
 
 def per_device(
     drafts,
@@ -107,6 +314,7 @@
             jnp.sum(jnp.where(child_order == 2 * parent + 1, places, 0)),
         ]
     ).astype(jnp.int32)
+    ids, all_routes, draft_rows = lax.optimization_barrier((ids, all_routes, draft_rows))
     attended = attend(drafts, keys, key_spans, ids, span_bias, groups, halves)
     term = jnp.dot(attended, out_weight, preferred_element_type=jnp.float32).astype(jnp.bfloat16)
     term = lax.psum_scatter(term, "tensor", scatter_dimension=0, tiled=True)
@@ -115,40 +323,44 @@
     mean_square = jnp.mean(merged * merged, axis=-1, keepdims=True)
     normed = (merged * lax.rsqrt(mean_square + 1e-05) * norm_gain).astype(jnp.bfloat16)
 
-    own = lax.all_gather(normed, "leaf", axis=0, tiled=True)
-    own = lax.all_gather(own, "expert", axis=0, tiled=True)
-    other = lax.ppermute(own, "tensor", swap)
-    merged_all = lax.all_gather(merged, "tensor", axis=0, tiled=True)
-
-    routes_at = all_routes.reshape(leaves, groups, halves, rows, 2).transpose(2, 1, 0, 3, 4)
-    routes_at = routes_at.reshape(halves, -1, 2)
-
-    def gate_of(block, which):
-        named = lax.dynamic_index_in_dim(routes_at, which, 0, keepdims=False)
-        logits = jnp.dot(block, router, preferred_element_type=jnp.float32)
-        hot = named[:, :, None] == jnp.arange(router.shape[1], dtype=jnp.int32)[None, None, :]
-        chosen = jnp.sum(jnp.where(hot, logits[:, None, :], 0.0), axis=-1)
-        gates = jax.nn.softmax(chosen, axis=-1)
-        return jnp.sum(jnp.where(named == expert, gates, 0.0), axis=-1, keepdims=True)
-
-    def hidden_of(block):
-        gate_v = jnp.dot(block, w_gate[0], preferred_element_type=jnp.float32)
-        up_v = jnp.dot(block, w_up[0], preferred_element_type=jnp.float32)
-        return (jax.nn.silu(gate_v) * up_v).astype(jnp.bfloat16)
-
-    own_gate = gate_of(own, half)
-    own_hidden = hidden_of(own)
-    other_gate = gate_of(other, 1 - half)
-    other_hidden = hidden_of(other)
-    other_part = (
-        jnp.dot(other_hidden, w_down[0], preferred_element_type=jnp.float32) * other_gate
-    ).astype(jnp.bfloat16)
-    returned = lax.ppermute(other_part, "tensor", swap)
-    own_part = jnp.dot(own_hidden, w_down[0], preferred_element_type=jnp.float32) * own_gate
-    part = (own_part + returned.astype(jnp.float32)).astype(jnp.bfloat16)
-    part = lax.psum_scatter(part, "expert", scatter_dimension=0, tiled=True)
-    part = lax.psum_scatter(part, "leaf", scatter_dimension=0, tiled=True)
-    mixed = lax.all_gather(part, "tensor", axis=0, tiled=True)
+    in_kernels = groups == 4 and halves == 2
+    if in_kernels:
+        every, merged_all = gather_rows(normed, merged, leaves, groups)
+    else:
+        every = lax.all_gather(normed, "leaf", axis=0, tiled=True)
+        every = lax.all_gather(every, "expert", axis=0, tiled=True)
+        every = lax.all_gather(every, "tensor", axis=0, tiled=True)
+        merged_all = lax.all_gather(merged, "tensor", axis=0, tiled=True)
+    every = every.reshape(-1, width)
+    merged_all = merged_all.reshape(-1, width)
+
+    named = all_routes.reshape(leaves, groups, halves, rows, 2).transpose(2, 1, 0, 3, 4)
+    named = named.reshape(-1, 2)
+    hot = named[:, :, None] == jnp.arange(router.shape[1], dtype=jnp.int32)[None, None, :]
+    logits = jnp.dot(every, router, preferred_element_type=jnp.float32)
+    chosen = jnp.sum(jnp.where(hot, logits[:, None, :], 0.0), axis=-1)
+    gates = jax.nn.softmax(chosen, axis=-1)
+    gate = jnp.sum(jnp.where(named == expert, gates, 0.0), axis=-1)
+    gate = gate.reshape(halves, -1, 1)
+
+    gate_v = jnp.dot(every, w_gate[0], preferred_element_type=jnp.float32)
+    up_v = jnp.dot(every, w_up[0], preferred_element_type=jnp.float32)
+    hidden = (jax.nn.silu(gate_v) * up_v).astype(jnp.bfloat16)
+    hidden = hidden.reshape(halves, -1, hidden.shape[1])
+
+    def product(which):
+        block = lax.dynamic_index_in_dim(hidden, which, 0, keepdims=False)
+        scale = lax.dynamic_index_in_dim(gate, which, 0, keepdims=False)
+        return jnp.dot(block, w_down[0], preferred_element_type=jnp.float32) * scale
+
+    returned = lax.ppermute(product(1 - half).astype(jnp.bfloat16), "tensor", swap)
+    part = (product(half) + returned.astype(jnp.float32)).astype(jnp.bfloat16)
+    if in_kernels:
+        mixed = scatter_rows(part, leaves, groups).reshape(-1, width)
+    else:
+        part = lax.psum_scatter(part, "expert", scatter_dimension=0, tiled=True)
+        part = lax.psum_scatter(part, "leaf", scatter_dimension=0, tiled=True)
+        mixed = lax.all_gather(part, "tensor", axis=0, tiled=True)
     return merged_all + mixed.astype(jnp.float32)
 
 

time: 487 us -> 372 us (0.76); the launches traced: 487 us -> 365 us
  waiting for transfers between devices: 303 us -> 60 us
  Pallas kernels: 6.16 us -> 149 us
  blocking collectives: 69.3 us -> 54.7 us
  matrix products: 85.1 us -> 72.7 us
  starting transfers between devices: 0.29 us -> 5.7 us
    pallas_call x0 -> x2, Pallas kernels: none -> 143 us  [the longest x1 82.8 us: scatter_rows(): pl.pallas_call(lambda *refs: scatter_kernel(leaves, rows, *refs), out_sha...]
    all_gather x3 -> x0, waiting for transfers between devices: 116 us -> none  [the longest x1 70.8 us: per_device(): own = lax.all_gather(own, 'expert', axis=0, tiled=True)]
    reduce_scatter x2 -> x0, waiting for transfers between devices: 104 us -> none  [the longest x1 66.6 us: per_device(): part = lax.psum_scatter(part, 'expert', scatter_dimension=0, tiled=True)]
    all_gather x1, waiting for transfers between devices: 49.6 us -> 4.69 us  [per_device(): keys = lax.all_gather(children, 'leaf', axis=0, tiled=True)]
    dot_general x8 -> x5, matrix products: 77 us -> 64.6 us  [the longest x2 23.5 us: product(): return jnp.dot(block, w_down[0], preferred_element_type=jnp.float32) * scale]
    all_to_all x1 -> x0, blocking collectives: 12.1 us -> none  [per_device(): lax.all_to_all(drafts, ('expert', 'tensor'), split_axis=0, concat_axis=1,...]
    reduce_scatter x1, waiting for transfers between devices: 23.1 us -> 35.1 us  [per_device(): term = lax.psum_scatter(term, 'expert', scatter_dimension=0, tiled=True)]
    ppermute x2 -> x1, waiting for transfers between devices: 0.01 us -> 9.79 us  [per_device(): lax.ppermute(product(1 - half).astype(jnp.bfloat16), 'tensor', swap)]
  transfers between devices with their start and end apart: 10 -> 5, of which waited for: 8 -> 4; matrix products, arithmetic and copies ran while one was open for 6% -> 1% of each run, Pallas kernels for 0% -> 0%
where the time goes in v2:
time: 372 us; the launch traced here: 365 us
  Pallas kernels  149 us (40%)
  matrix products  72.7 us (20%)
  waiting for transfers between devices  60 us (16%)
  blocking collectives  54.7 us (15%)
  between operations  13.3 us (4%)
  other arithmetic  8.78 us (2%)
  starting transfers between devices  5.7 us (2%)
    pallas_call x1, Pallas kernels, scatter_rows(): pl.pallas_call(lambda *refs: scatter_kernel(leaves, rows, *refs), out_sha...  82.8 us
    pallas_call x1, Pallas kernels, gather_rows(): pl.pallas_call(lambda *refs: gather_kernel(leaves, rows, *refs), out_shap...  60.1 us
    all_gather x1, blocking collectives, per_device(): all_routes = lax.all_gather(routes, ('leaf', 'expert'), axis=0, tiled=True)  42.3 us
    reduce_scatter x1, waiting for transfers between devices, per_device(): term = lax.psum_scatter(term, 'expert', scatter_dimension=0, tiled=True)  35.1 us
    dot_general x2, matrix products, product(): return jnp.dot(block, w_down[0], preferred_element_type=jnp.float32) * scale  23.5 us
    dot_general x1, matrix products, per_device(): up_v = jnp.dot(every, w_up[0], preferred_element_type=jnp.float32)  17.4 us
    dot_general x1, matrix products, per_device(): gate_v = jnp.dot(every, w_gate[0], preferred_element_type=jnp.float32)  15.8 us
    all_gather x1, blocking collectives, per_device(): lax.all_gather(spans, 'leaf', axis=0, tiled=True).reshape(-1, 1, R)  12.4 us
  transfers between devices with their start and end apart: 5, of which 4 were waited for; matrix products, arithmetic and copies ran while one was open for 1% of the time, Pallas kernels for 0%

profile of v2, /device:TPU:0, one launch (start us, length us, event | category | flops | bytes accessed | tf_op | source)
XLA Modules:
  0.0 364.9 jit_solution(14758958117312658293)
XLA Ops:
  6.5 0.0 copy-start
  6.5 0.0 all-gather.4.cloned.1.call-start
  6.5 0.7 all-gather.4.cloned.1.call-update
  7.3 5.2 %all-to-all-start = ((bf16[8,32,768]{2,1,0:T(8,128)(2,1)}), bf16[8,32,768]{2,1,0:T(8,128)(2,1)S(1)}, u32[]{:S(2)}, u32[]{:S(2)}) async-start(bf16[8,32,768]{2,1,0:T(8,128)(2,1)} %bitcast.61), calls=%async_computation | async-start | bytes 786432 | tf_op jit(solution)/shard_map/all_to_all | solution.py:307
  12.4 0.0 reduce-scatter.3.cloned.1.call-start
  12.5 42.3 %all-gather = s32[16,64,2]{1,2,0:T(2,128)S(1)} all-gather(s32[1,64,2]{1,2,0:T(2,128)} %bitcast.69), channel_id=1, replica_groups=mesh['leaf'=4,'expert'=4,'tensor'=2] {'leaf','expert'}, dimensions={0}, use_global_device_ids=true | all-gather | bytes 8704 | tf_op jit(solution)/shard_map/all_gather | solution.py:306
  54.8 0.1 reshape.57
  54.8 12.4 %all-gather.1 = s32[4,1,512]{2,1,0:T(1,128)} all-gather(s32[1,1,512]{2,1,0:T(1,128)} %bitcast.66), channel_id=1, replica_groups=mesh['leaf'=4,'expert'=4,'tensor'=2] {'leaf'}, dimensions={0}, use_global_device_ids=true | all-gather | bytes 10240 | tf_op jit(solution)/shard_map/all_gather | solution.py:305
  67.3 1.4 fusion.21
  68.7 1.9 pad_add_fusion.refs_0_
  70.6 0.0 all-to-all-done
  70.6 4.7 %all-gather.4.cloned.1.call-done.refs_3_.refs_4_ = bf16[2048,768]{1,0:T(8,128)(2,1)} async-done(((bf16[512,768]{1,0:T(8,128)(2,1)}), bf16[2048,768]{1,0:T(8,128)(2,1)}) %all-gather.4.cloned.1.call-update) | async-done | bytes 3145744 | tf_op jit(solution)/shard_map/all_gather | solution.py:304
  75.3 6.2 %shard_map.118 = bf16[256,768]{1,0:T(8,128)(2,1)} custom-call(s32[2]{0:T(128)} %pad_add_fusion.refs_0_, f32[6,16]{1,0:T(8,128)} %refs_1_.1, bf16[256,768]{1,0:T(8,128)(2,1)} %refs_2_.1, bf16[2048,768]{1,0:T(8,128)(2,1)} %all-gather.4.cloned.1.call-done.refs_3_.refs_4_, bf16[2048,768]{1,0:T(8,128)(2,1)} %all-gather.4.cloned.1.call-done.refs_3_.refs_4_, ...), custom_call_target="tpu_custom_call" | custom-call | flops 402653184 | bytes 1572864 | tf_op jit(solution)/shard_map/pallas_call | solution.py:51
  81.5 0.0 copy-start.4
  81.5 8.1 %convolution_convert_fusion = bf16[256,6144]{1,0:T(8,128)(2,1)} fusion(bf16[256,768]{1,0:T(8,128)(2,1)} %shard_map.118, bf16[768,6144]{1,0:T(8,128)(2,1)} %param.17), kind=kOutput, calls=%fused_computation.10 | convolution fusion | flops 2417491968 | bytes 12976128 | tf_op jit(solution)/shard_map/dot_general | solution.py:319
  89.6 0.0 reduce-scatter.3.cloned.1.call-update
  89.6 0.0 reduce-scatter.5.cloned.1.call-start
  89.7 9.6 %reduce-scatter.3.cloned.1.call-done = bf16[128,6144]{1,0:T(8,128)(2,1)} async-done(((bf16[256,6144]{1,0:T(8,128)(2,1)}), bf16[128,6144]{1,0:T(8,128)(2,1)}) %reduce-scatter.3.cloned.1.call-update) | async-done | bytes 1572880 | tf_op jit(solution)/shard_map/reduce_scatter | solution.py:320
  99.3 0.0 reduce-scatter.5.cloned.1.call-update
  99.3 0.1 reshape.54
  99.4 0.1 eq.40
  99.5 35.1 %reduce-scatter.5.cloned.1.call-done = bf16[32,6144]{1,0:T(8,128)(2,1)} async-done(((bf16[128,6144]{1,0:T(8,128)(2,1)}), bf16[32,6144]{1,0:T(8,128)(2,1)}) %reduce-scatter.5.cloned.1.call-update) | async-done | bytes 393232 | tf_op jit(solution)/shard_map/reduce_scatter | solution.py:321
  134.7 2.1 convert_add_fusion.1
  136.8 0.0 copy-done.4
  136.8 1.9 multiply_convert_fusion.2.refs_0_
  138.7 60.1 %shard_map.119 = (bf16[2,512,6144]{2,1,0:T(8,128)(2,1)}, f32[2,32,6144]{2,1,0:T(8,128)}) custom-call(bf16[32,6144]{1,0:T(8,128)(2,1)} %multiply_convert_fusion.2.refs_0_, f32[32,6144]{1,0:T(8,128)} %get-tuple-element.17.refs_1_), custom_call_target="tpu_custom_call" | custom-call | tf_op jit(solution)/shard_map/pallas_call | solution.py:173
  198.8 0.0 copy-done
  198.8 7.9 %fusion.23 = f32[1024,4]{0,1:T(4,128)S(1)} fusion(bf16[1024,6144]{1,0:T(8,128)(2,1)} %bitcast.56, bf16[6144,4]{0,1:T(4,128)(2,1)S(1)} %copy-done), kind=kOutput, calls=%fused_computation.36 | convolution fusion | flops 50331648 | bytes 12648448 | tf_op jit(solution)/shard_map/dot_general | solution.py:340
  206.8 0.1 sub.18
  206.9 0.1 reduce_sum.60
  207.0 0.1 div.24
  207.1 0.1 reshape.55
  207.2 0.0 copy-start.2
  207.2 17.4 %fusion.4 = f32[1024,1024]{1,0:T(8,128)S(1)} fusion(bf16[1024,6144]{1,0:T(8,128)(2,1)} %bitcast.57, bf16[1,6144,1024]{2,1,0:T(8,128)(2,1)} %param.22), kind=kOutput, calls=%fused_computation.4 | convolution fusion | flops 12884901888 | bytes 29360128 | tf_op jit(solution)/shard_map/dot_general | solution.py:347
  224.6 0.0 copy-done.2
  224.6 15.8 %multiply_convert_fusion.1 = bf16[1024,1024]{1,0:T(8,128)(2,1)S(1)} fusion(f32[1024,1024]{1,0:T(8,128)S(1)} %fusion.4, bf16[1024,6144]{1,0:T(8,128)(2,1)S(1)} %bitcast.58, bf16[1,6144,1024]{2,1,0:T(8,128)(2,1)} %param.21), kind=kOutput, calls=%fused_computation.11 | convolution fusion | flops 12891193344 | bytes 31457280 | tf_op jit(solution)/shard_map/dot_general | solution.py:346
  240.4 11.5 %multiply_convert_fusion = bf16[512,6144]{1,0:T(8,128)(2,1)S(1)} fusion(bf16[1,1024,6144]{2,1,0:T(8,128)(2,1)} %param.23, f32[512]{0:T(512)S(1)} %bitcast.68, bf16[2,512,1024]{2,1,0:T(8,128)(2,1)S(1)} %bitcast.70, s32[]{:T(128)S(6)} %select_n.31), kind=kOutput, calls=%fused_computation.9 | convolution fusion | flops 6448742400 | bytes 19924996 | tf_op jit(solution)/shard_map/dot_general | solution.py:354
  251.9 0.4 collective-permute-start
  252.4 9.8 %collective-permute-done = bf16[512,6144]{1,0:T(8,128)(2,1)S(1)} collective-permute-done((bf16[512,6144]{1,0:T(8,128)(2,1)S(1)}, bf16[512,6144]{1,0:T(8,128)(2,1)S(1)}, u32[]{:S(2)}, u32[]{:S(2)}) %collective-permute-start) | collective-permute-done | bytes 6291488 | tf_op jit(solution)/shard_map/ppermute | solution.py:356
  262.2 0.0 copy-start.3
  262.2 0.0 copy-start.1
  262.2 12.0 %add_convert_fusion.refs_0_ = bf16[512,6144]{1,0:T(8,128)(2,1)S(1)} fusion(bf16[512,6144]{1,0:T(8,128)(2,1)S(1)} %collective-permute-done, bf16[1,1024,6144]{2,1,0:T(8,128)(2,1)} %param.23, f32[512]{0:T(512)S(1)} %bitcast.67, bf16[2,512,1024]{2,1,0:T(8,128)(2,1)S(1)} %bitcast.71, s32[]{:T(128)S(6)} %select_n.28), kind=kOutput, calls=%fused_computation.8 | convolution fusion | flops 6455033856 | bytes 26216452 | tf_op jit(solution)/shard_map/dot_general | solution.py:354
  274.2 82.8 %shard_map.120 = bf16[2,32,6144]{2,1,0:T(8,128)(2,1)S(1)} custom-call(bf16[512,6144]{1,0:T(8,128)(2,1)S(1)} %add_convert_fusion.refs_0_), custom_call_target="tpu_custom_call" | custom-call | tf_op jit(solution)/shard_map/pallas_call | solution.py:263
  357.0 0.0 copy-done.3
  357.0 1.3 convert_add_fusion
  358.4 0.0 copy-done.1
  (9 shorter events, 0.2 us)
Async XLA Ops:
  6.5 192.2 %copy-start = (bf16[6144,4]{0,1:T(4,128)(2,1)S(1)}, bf16[6144,4]{0,1:T(4,128)(2,1)}, u32[]{:S(2)}) copy-start(bf16[6144,4]{0,1:T(4,128)(2,1)} %param.19) | copy-start | bytes 147460
  6.5 68.8 %all-gather.4.cloned.1.call-start = ((), (), s32[]{:S(2)}) async-start(), calls=%async_computation.3 | async-start | bytes 3932160 | tf_op jit(solution)/shard_map/all_gather | solution.py:304
  7.3 63.3 %all-to-all-start = ((bf16[8,32,768]{2,1,0:T(8,128)(2,1)}), bf16[8,32,768]{2,1,0:T(8,128)(2,1)S(1)}, u32[]{:S(2)}, u32[]{:S(2)}) async-start(bf16[8,32,768]{2,1,0:T(8,128)(2,1)} %bitcast.61), calls=%async_computation | async-start | bytes 786432 | tf_op jit(solution)/shard_map/all_to_all | solution.py:307
  12.4 86.8 %reduce-scatter.3.cloned.1.call-start = ((), (), s32[]{:S(2)}) async-start(), calls=%async_computation.4 | async-start | bytes 4718592 | tf_op jit(solution)/shard_map/reduce_scatter | solution.py:320
  81.5 55.3 %copy-start.4 = (f32[6144]{0:T(1024)S(1)}, f32[6144]{0:T(1024)}, u32[]{:S(2)}) copy-start(f32[6144]{0:T(1024)} %param.18) | copy-start | bytes 73732
  89.6 45.0 %reduce-scatter.5.cloned.1.call-start = ((), (), s32[]{:S(2)}) async-start(), calls=%async_computation.5 | async-start | bytes 1966080 | tf_op jit(solution)/shard_map/reduce_scatter | solution.py:321
  207.2 17.4 %copy-start.2 = (bf16[2,512,6144]{2,1,0:T(8,128)(2,1)S(1)}, bf16[2,512,6144]{2,1,0:T(8,128)(2,1)}, u32[]{:S(2)}) copy-start(bf16[2,512,6144]{2,1,0:T(8,128)(2,1)} %get-tuple-element.13) | copy-start | bytes 37748740
  251.9 10.2 %collective-permute-start = (bf16[512,6144]{1,0:T(8,128)(2,1)S(1)}, bf16[512,6144]{1,0:T(8,128)(2,1)S(1)}, u32[]{:S(2)}, u32[]{:S(2)}) collective-permute-start(bf16[512,6144]{1,0:T(8,128)(2,1)S(1)} %multiply_convert_fusion), channel_id=1, source_target_pairs={{0,1},{1,0},{2,3},{3,2},{4,5},{5,4},{6,7},{7,6},{8,9},{9,8},{10,11... | collective-permute-start | bytes 18874376 | tf_op jit(solution)/shard_map/ppermute | solution.py:356
  262.2 94.8 %copy-start.3 = (f32[2,32,6144]{2,1,0:T(8,128)S(1)}, f32[2,32,6144]{2,1,0:T(8,128)}, u32[]{:S(2)}) copy-start(f32[2,32,6144]{2,1,0:T(8,128)} %get-tuple-element.12) | copy-start | bytes 4718596
  262.2 96.2 %copy-start.1 = (bf16[6144,4]{0,1:T(4,128)(2,1)S(1)}, bf16[6144,4]{0,1:T(4,128)(2,1)}, u32[]{:S(2)}) copy-start(bf16[6144,4]{0,1:T(4,128)(2,1)} %param.19) | copy-start | bytes 147460
Sparse Core Ops, SparseCore 0:
  8.9 66.3 all-gather.3
  89.8 9.4 reduce-scatter.2
  102.6 32.0 reduce-scatter.4
